TPU v7x, 256 devices: a whole 4x4x8 slice. The times are simulated.
256 devices in a mesh: dev: 256 (over x, y, z, core).
Axes of the slice: x: 4, y: 4, z: 8, core: 2. Of those that a mesh axis runs over, the one named last changes fastest.
Arguments:
- state: float32 [5, 8, 8, 8, 32768], P(None, None, None, None, 'dev'), may hold values from -1 to 5, as said below
- neighbours: int32 [6, 32768], P(None, 'dev'), may hold values from 0 to 32767, as said below
Outputs:
- change: float32 [5, 8, 8, 8, 32768], P(None, None, None, None, 'dev')
Inputs may be any that keep to these rules, and one draw needn't show every extreme that they name: `state`: component 0 is the density, 1 to 3 the momentum, 4 the total energy of an ideal gas with ratio of heats 1.4; at every node density and pressure lie between 0.6 and 1.8 and each velocity component between -0.4 and 0.4. `neighbours`: device i holds elements i * 128 to (i + 1) * 128 - 1. Across face 2a+1 of element e lies element n exactly when across face 2a of n lies e. Neighbours across faces 0 and 1 lie on the element's own device; across faces 2 and 3 on its own device or on the device whose index differs from it in the lowest bit; across face 5 on the device with index + 2 and across face 4 on the device with index - 2, cyclically. Of one device's faces 2 exactly 8 have their neighbour on another device, and likewise of its faces 3.
All inputs are finite; a program needn't handle non-finite values.
Results may differ from a plain program's by a relative error of at most 0.0001.
Values sent between devices are 32-bit elements; how exact they have to be, the bound alone decides.
A program may use at most 128 MiB of HBM per device.

v0:
```python
import jax
import jax.numpy as jnp
import numpy as np
from jax import lax
from jax.sharding import PartitionSpec as P

LX = 8


GAMMA = 1.4
STEP = 0.003
FORMS = ("ai,nijke->najke", "bj,nijke->nibke", "ck,nijke->nijce")
LOBATTO_EIGHT = (
    -1.0,
    -0.8717401485096066,
    -0.5917001814331423,
    -0.2092992179024789,
    0.2092992179024789,
    0.5917001814331423,
    0.8717401485096066,
    1.0,
)


def from_partner(block, axis, bit):
    count = lax.axis_size(axis)
    route = []
    for low in range(count):
        high = low | 1 << bit
        if high != low and high < count:
            route += [(low, high), (high, low)]
    return lax.ppermute(block, axis, route)


def passed_along(array, axis, by):
    devices = lax.axis_size(axis)
    return lax.ppermute(array, axis, [(i, (i + by) % devices) for i in range(devices)])


def lobatto_deriv(points_count):
    points = np.array(LOBATTO_EIGHT)
    identity = np.eye(points_count)
    spacing = points[:, None] - points[None, :] + identity
    weights = 1.0 / np.prod(spacing, axis=1)
    matrix = weights[None, :] / weights[:, None] / spacing
    matrix = matrix * (1.0 - identity)
    matrix = matrix - identity * np.sum(matrix, axis=1)[:, None]
    return jnp.asarray(matrix, dtype=jnp.float32)


def primitive(state):
    density = state[0]
    momentum = state[1:4]
    velocity = momentum / density
    pressure = (GAMMA - 1.0) * (state[4] - 0.5 * jnp.sum(momentum * velocity, axis=0))
    return (density, momentum, velocity, pressure)


def flux_rows(state, momentum, velocity, pressure, normal):
    speed_n = velocity[normal]
    rows = [momentum[normal]]
    for column in range(3):
        term = momentum[column] * speed_n
        if column == normal:
            term = term + pressure
        rows.append(term)
    rows.append((state[4] + pressure) * speed_n)
    return jnp.stack(rows)


def normal_flux(state, normal):
    density, momentum, velocity, pressure = primitive(state)
    fluxes = flux_rows(state, momentum, velocity, pressure, normal)
    wave = jnp.abs(velocity[normal]) + jnp.sqrt(GAMMA * pressure / density)
    return (fluxes, wave)


def rusanov(left, right, normal):
    flux_left, wave_left = normal_flux(left, normal)
    flux_right, wave_right = normal_flux(right, normal)
    wave = jnp.maximum(wave_left, wave_right)
    return 0.5 * (flux_left + flux_right) - 0.5 * wave * (right - left)


def face(field, normal, sided):
    return lax.index_in_dim(field, sided * (field.shape[1] - 1), 1 + normal, keepdims=False)


def volume_part(state, deriv):
    density, momentum, velocity, pressure = primitive(state)
    rate = jnp.zeros_like(state)
    own_lower = []
    own_upper = []
    for normal in range(3):
        fluxes = flux_rows(state, momentum, velocity, pressure, normal)
        rate = rate - jnp.einsum(FORMS[normal], deriv, fluxes, precision=lax.Precision.HIGHEST)
        own_lower.append(face(fluxes, normal, 0))
        own_upper.append(face(fluxes, normal, 1))
    return (rate, own_lower, own_upper)


def add_surface(rate, own_lower, own_upper, lower_star, upper_star):
    last = rate.shape[1] - 1
    lift = last * (last + 1) / 2.0
    for normal in range(3):
        upper_idx = (slice(None),) * (1 + normal) + (last,)
        lower_idx = (slice(None),) * (1 + normal) + (0,)
        rate = rate.at[upper_idx].add(lift * (own_upper[normal] - upper_star[normal]))
        rate = rate.at[lower_idx].add(lift * (lower_star[normal] - own_lower[normal]))
    return rate


def take_cols(table, columns):
    return jnp.take(table, columns, axis=-1)


def ranks(valid, keys):
    before = (keys[None, :] < keys[:, None]) & valid[None, :]
    return jnp.sum(before.astype(jnp.int32), axis=1)


def slot_index(valid, order, slots):
    total = valid.shape[0]
    hits = (order[None, :] == jnp.arange(slots, dtype=jnp.int32)[:, None]) & valid[None, :]
    return jnp.sum(jnp.where(hits, jnp.arange(total, dtype=jnp.int32)[None, :], 0), axis=1)


def tendency(state, neighbours, deriv, device):
    total = state.shape[-1]
    local_ids = neighbours % total
    remote = neighbours // total != device
    serial = jnp.arange(total, dtype=jnp.int32)
    rate, own_lower, own_upper = volume_part(state, deriv)
    lower = [face(state, normal, 0) for normal in range(3)]
    upper = [face(state, normal, 1) for normal in range(3)]
    rank_low = jnp.clip(ranks(remote[2], local_ids[2]), 0, LX - 1)
    rank_up = jnp.clip(ranks(remote[3], local_ids[3]), 0, LX - 1)
    send_low = slot_index(remote[2], ranks(remote[2], serial), LX)
    send_up = slot_index(remote[3], ranks(remote[3], serial), LX)
    plus_x = rusanov(upper[0], take_cols(lower[0], local_ids[1]), 0)
    minus_x = take_cols(plus_x, local_ids[0])
    arrived = from_partner(take_cols(lower[1], send_low), "dev", 0)
    across_y = jnp.where(remote[3], take_cols(arrived, rank_up), take_cols(lower[1], local_ids[3]))
    plus_y = rusanov(upper[1], across_y, 1)
    returned = from_partner(take_cols(plus_y, send_up), "dev", 0)
    minus_y = jnp.where(remote[2], take_cols(returned, rank_low), take_cols(plus_y, local_ids[2]))
    above = passed_along(lower[2], "dev", -2)
    plus_z = rusanov(upper[2], take_cols(above, local_ids[5]), 2)
    below = passed_along(plus_z, "dev", 2)
    minus_z = take_cols(below, local_ids[4])
    return add_surface(
        rate, own_lower, own_upper, [minus_x, minus_y, minus_z], [plus_x, plus_y, plus_z]
    )


def body(state, neighbours):
    deriv = lobatto_deriv(state.shape[1])
    device = lax.axis_index("dev")
    rate_start = tendency(state, neighbours, deriv, device)
    first = state + STEP * rate_start
    rate_first = tendency(first, neighbours, deriv, device)
    return 0.5 * STEP * (rate_start + rate_first)


def solution(mesh):
    in_specs = (P(None, None, None, None, "dev"), P(None, "dev"))
    out_specs = P(None, None, None, None, "dev")
    return jax.shard_map(body, mesh=mesh, in_specs=in_specs, out_specs=out_specs, check_vma=False)
```

profile of v0, /device:TPU:1, one launch (start us, length us, event | category | flops | bytes accessed | tf_op | source)
XLA Modules:
  0.0 258.9 jit_solution(18425897157408662711)
XLA Ops:
  0.0 2.8 %fusion.154 = (f32[5,8,8,1,128]{4,3,2,1,0:T(1,128)}, f32[5,8,8,1,128]{4,3,2,1,0:T(1,128)}) fusion(f32[5,8,8,8,128]{4,3,2,1,0:T(8,128)} %param.33), kind=kLoop, calls=%fused_computation.475 | loop fusion | bytes 655360 | tf_op jit(solution)/shard_map/slice | solution.py:86
  2.8 11.1 %collective-permute-start.2 = (f32[5,8,8,128]{3,2,1,0:T(8,128)}, f32[5,8,8,128]{3,2,1,0:T(8,128)}, u32[]{:S(2)}, u32[]{:S(2)}) collective-permute-start(f32[5,8,8,128]{3,2,1,0:T(8,128)} %bitcast.83), channel_id=1, source_target_pairs={{0,254},{1,255},{2,0},{3,1},{4,2},{5,3},{6,4},{7,5},{8,6},{9,7},{1... | collective-permute-start | bytes 491528 | tf_op jit(solution)/shard_map/ppermute | solution.py:37
  39.9 2.5 copy.1053
  54.9 2.5 gather_fusion.1
  57.6 2.5 copy.1071
  67.6 2.6 %gather_fusion.4 = f32[128,5,8,8]{3,2,1,0:T(8,128)S(1)} fusion(f32[5,8,8,128]{2,1,3,0:T(8,128)} %bitcast.1053, s32[1024]{0:T(1024)S(1)} %get-tuple-element.321), kind=kCustom, calls=%fused_computation.4.clone | custom fusion | bytes 328192 | tf_op jit(solution)/shard_map/jit(_take)/gather | solution.py:114
  79.1 2.5 gather_fusion.7
  92.5 2.5 gather_fusion.8
  95.0 2.5 copy.1121
  100.2 5.0 %scatter-add.46 = f32[5,8,8,8,128]{4,3,2,0,1:T(8,128)} dynamic-update-slice(f32[5,8,8,8,128]{4,3,2,0,1:T(8,128)} %copy_dynamic-update-slice_fusion.8, f32[5,8,8,1,128]{4,3,2,0,1:T(1,128)S(1)} %copy.1126, s32[]{:T(128)} %constant.365.clone.1, s32[]{:T(128)} %constant.365.clone.1, s32[]{:T(128)} %constant.365.clone.1, s32[]{:T(128)} %constant.370.clone.1, s32[]{:T(128)} %constant.365.clone.1) | dynamic-update-slice | bytes 327684 | tf_op jit(solution)/shard_map/scatter-add | solution.py:108
  106.6 4.1 %collective-permute-done.3 = f32[5,8,8,128]{3,1,2,0:T(8,128)S(1)} collective-permute-done((f32[5,8,8,128]{3,1,2,0:T(8,128)S(1)}, f32[5,8,8,128]{3,1,2,0:T(8,128)S(1)}, u32[]{:S(2)}, u32[]{:S(2)}) %collective-permute-start.3) | collective-permute-done | bytes 163872 | tf_op jit(solution)/shard_map/ppermute | solution.py:37
  117.6 5.0 %scatter-add.49 = f32[5,8,8,8,128]{4,3,2,0,1:T(8,128)} dynamic-update-slice(f32[5,8,8,8,128]{4,3,2,0,1:T(8,128)} %scatter-add.46, f32[5,8,8,1,128]{4,3,2,0,1:T(1,128)S(1)} %copy.1131, s32[]{:T(128)} %constant.365.clone.1, s32[]{:T(128)} %constant.365.clone.1, s32[]{:T(128)} %constant.365.clone.1, s32[]{:T(128)} %constant.365.clone.1, s32[]{:T(128)} %constant.365.clone.1) | dynamic-update-slice | bytes 327684 | tf_op jit(solution)/shard_map/scatter-add | solution.py:109
  122.6 2.8 %copy_add_fusion = f32[5,8,8,8,128]{4,1,0,2,3:T(8,128)S(1)} fusion(f32[5,8,8,8,128]{4,3,2,1,0:T(8,128)S(1)} %copy-done.1, f32[5,8,8,8,128]{4,3,2,0,1:T(8,128)} %scatter-add.49), kind=kLoop, calls=%fused_computation.33 | loop fusion | flops 655360 | bytes 3932160 | tf_op jit(solution)/shard_map/add | solution.py:160
  130.1 2.8 %collective-permute-start.6 = (f32[5,8,8,128]{3,1,0,2:T(8,128)}, f32[5,8,8,128]{3,1,0,2:T(8,128)}, u32[]{:S(2)}, u32[]{:S(2)}) collective-permute-start(f32[5,8,8,128]{3,1,0,2:T(8,128)} %slice_bitcast_fusion.6), channel_id=1, source_target_pairs={{0,254},{1,255},{2,0},{3,1},{4,2},{5,3},{6,4},{7,5},{8,6},{9,7},{1... | collective-permute-start | bytes 491528 | tf_op jit(solution)/shard_map/ppermute | solution.py:37
  148.9 4.3 %gather_fusion.10 = f32[128,5,8,8]{3,2,1,0:T(8,128)} fusion(f32[5,8,8,128]{2,1,3,0:T(8,128)} %bitcast.1055, s32[1024]{0:T(1024)} %copy-done.59), kind=kCustom, calls=%fused_computation.8.clone | custom fusion | bytes 328192 | tf_op jit(solution)/shard_map/jit(_take)/gather | solution.py:114
  153.2 2.5 copy.1174
  159.3 4.3 %gather_fusion.11 = f32[128,5,8,8]{3,2,1,0:T(8,128)} fusion(f32[5,8,8,128]{2,1,3,0:T(8,128)} %copy.1180, s32[1024]{0:T(1024)} %get-tuple-element.322), kind=kCustom, calls=%fused_computation.9.clone | custom fusion | bytes 328192 | tf_op jit(solution)/shard_map/jit(_take)/gather | solution.py:114
  163.5 3.1 %copy.1181 = f32[128,5,8,8]{0,2,1,3:T(8,128)} copy(f32[128,5,8,8]{3,2,1,0:T(8,128)} %gather_fusion.11) | data formatting | bytes 327680 | tf_op jit(solution)/shard_map/jit(_take)/gather | solution.py:114
  171.7 3.3 %fusion.5 = f32[5,8,8,128,8]{3,4,2,1,0:T(8,128)S(1)} fusion(f32[8,8,1,1,1]{1,0,4,3,2:T(8,128)S(1)} %copy-done.48, f32[5,8,8,8,128]{4,1,0,2,3:T(8,128)} %get-tuple-element.191), kind=kOutput, calls=%fused_computation.27 | convolution fusion | flops 31457280 | bytes 2621696 | tf_op jit(solution)/shard_map/ck,nijke->nijce/dot_general | solution.py:96
  175.0 3.6 %fusion.3 = f32[5,8,8,8,128]{4,2,0,3,1:T(8,128)S(1)} fusion(f32[8,8,1,1,1]{1,0,2,4,3:T(8,128)S(1)} %copy-done.50, f32[5,8,8,128,8]{3,4,2,1,0:T(8,128)S(1)} %fusion.5, f32[5,8,8,8,128]{4,1,0,2,3:T(8,128)} %get-tuple-element.190, f32[5,8,8,128,8]{3,4,2,1,0:T(8,128)S(1)} %fusion.8), kind=kOutput, calls=%fused_computation.25 | convolution fusion | flops 32440320 | bytes 5243136 | tf_op jit(solution)/shard_map/bj,nijke->nibke/dot_general | solution.py:96
  181.0 4.3 %gather_fusion.14 = f32[128,5,8,8]{3,2,1,0:T(8,128)} fusion(f32[5,8,8,128]{2,1,3,0:T(8,128)} %copy.1192, s32[1024]{0:T(1024)} %copy-done.60), kind=kCustom, calls=%fused_computation.10.clone | custom fusion | bytes 328192 | tf_op jit(solution)/shard_map/jit(_take)/gather | solution.py:114
  188.6 2.5 gather_fusion.13
  191.1 2.7 %copy.1194 = f32[128,5,8,8]{0,2,3,1:T(8,128)S(1)} copy(f32[128,5,8,8]{3,2,1,0:T(8,128)} %gather_fusion.13) | data formatting | bytes 327680 | tf_op jit(solution)/shard_map/jit(_take)/gather | solution.py:114
  200.9 4.3 %gather_fusion.17 = f32[128,5,8,8]{3,2,1,0:T(8,128)} fusion(f32[5,8,8,128]{2,1,3,0:T(8,128)} %copy.1203, s32[1024]{0:T(1024)} %get-tuple-element.320), kind=kCustom, calls=%fused_computation.11.clone | custom fusion | bytes 328192 | tf_op jit(solution)/shard_map/jit(_take)/gather | solution.py:114
  207.6 3.2 %scatter-add.54 = f32[5,8,8,8,128]{4,2,0,1,3:T(8,128)S(1)} dynamic-update-slice(f32[5,8,8,8,128]{4,2,0,1,3:T(8,128)S(1)} %fusion.36, f32[5,8,1,8,128]{4,2,0,1,3:T(1,128)S(1)} %slice_add_fusion.2, s32[]{:T(128)} %constant.365.clone.1, s32[]{:T(128)} %constant.365.clone.1, s32[]{:T(128)} %constant.370.clone.1, s32[]{:T(128)} %constant.365.clone.1, s32[]{:T(128)} %constant.365.clone.1) | dynamic-update-slice | bytes 327684 | tf_op jit(solution)/shard_map/scatter-add | solution.py:108
  210.8 2.5 gather_fusion.16
  216.9 3.2 %scatter-add.55 = f32[5,8,8,8,128]{4,2,0,1,3:T(8,128)S(1)} dynamic-update-slice(f32[5,8,8,8,128]{4,2,0,1,3:T(8,128)S(1)} %scatter-add.54, f32[5,8,1,8,128]{4,2,0,1,3:T(1,128)S(1)} %slice_add_fusion.1, s32[]{:T(128)} %constant.365.clone.1, s32[]{:T(128)} %constant.365.clone.1, s32[]{:T(128)} %constant.365.clone.1, s32[]{:T(128)} %constant.365.clone.1, s32[]{:T(128)} %constant.365.clone.1) | dynamic-update-slice | bytes 327684 | tf_op jit(solution)/shard_map/scatter-add | solution.py:109
  220.1 3.1 %copy.1216 = f32[5,8,8,128]{2,1,3,0:T(8,128)} copy(f32[5,8,8,128]{3,1,0,2:T(8,128)} %collective-permute-done.6) | data formatting | bytes 327680 | tf_op jit(solution)/shard_map/ppermute | solution.py:37
  223.2 4.3 %gather_fusion.18 = f32[128,5,8,8]{3,2,1,0:T(8,128)} fusion(f32[5,8,8,128]{2,1,3,0:T(8,128)} %copy.1216, s32[1024]{0:T(1024)} %pad_clamp_fusion.1), kind=kCustom, calls=%fused_computation.12.clone | custom fusion | bytes 328192 | tf_op jit(solution)/shard_map/jit(_take)/gather | solution.py:114
  232.8 9.8 %collective-permute-done.7 = f32[5,8,8,128]{3,1,0,2:T(8,128)S(1)} collective-permute-done((f32[5,8,8,128]{3,1,0,2:T(8,128)S(1)}, f32[5,8,8,128]{3,1,0,2:T(8,128)S(1)}, u32[]{:S(2)}, u32[]{:S(2)}) %collective-permute-start.7) | collective-permute-done | bytes 163872 | tf_op jit(solution)/shard_map/ppermute | solution.py:37
  244.8 4.3 %gather_fusion.19 = f32[128,5,8,8]{3,2,1,0:T(8,128)} fusion(f32[5,8,8,128]{2,1,3,0:T(8,128)} %copy.1228, s32[1024]{0:T(1024)} %copy-done.61), kind=kCustom, calls=%fused_computation.13.clone | custom fusion | bytes 328192 | tf_op jit(solution)/shard_map/jit(_take)/gather | solution.py:114
  252.7 3.2 %scatter-add.59 = f32[5,8,8,8,128]{4,3,2,0,1:T(8,128)S(1)} dynamic-update-slice(f32[5,8,8,8,128]{4,3,2,0,1:T(8,128)S(1)} %copy.1232, f32[5,8,8,1,128]{4,3,2,0,1:T(1,128)S(1)} %add.415, s32[]{:T(128)} %constant.365.clone.1, s32[]{:T(128)} %constant.365.clone.1, s32[]{:T(128)} %constant.365.clone.1, s32[]{:T(128)} %constant.365.clone.1, s32[]{:T(128)} %constant.365.clone.1) | dynamic-update-slice | bytes 327684 | tf_op jit(solution)/shard_map/scatter-add | solution.py:109
  (393 shorter events, 137.7 us)
Async XLA Ops:
  0.0 15.6 %copy-start.49 = (s32[6,128]{1,0:T(8,128)S(1)}, s32[6,128]{1,0:T(8,128)}, u32[]{:S(2)}) copy-start(s32[6,128]{1,0:T(8,128)} %param.34) | copy-start | bytes 9220
  2.8 88.0 %collective-permute-start.2 = (f32[5,8,8,128]{3,2,1,0:T(8,128)}, f32[5,8,8,128]{3,2,1,0:T(8,128)}, u32[]{:S(2)}, u32[]{:S(2)}) collective-permute-start(f32[5,8,8,128]{3,2,1,0:T(8,128)} %bitcast.83), channel_id=1, source_target_pairs={{0,254},{1,255},{2,0},{3,1},{4,2},{5,3},{6,4},{7,5},{8,6},{9,7},{1... | collective-permute-start | bytes 491528 | tf_op jit(solution)/shard_map/ppermute | solution.py:37
  15.6 4.6 %copy-start.51 = (pred[128]{0:T(512)(128)(4,1)}, pred[128]{0:T(512)(128)(4,1)S(1)}, u32[]{:S(2)}) copy-start(pred[128]{0:T(512)(128)(4,1)S(1)} %get-tuple-element.312) | copy-start | bytes 388
  18.0 4.6 %copy-start.66 = (pred[8]{0:T(512)(128)(4,1)}, pred[8]{0:T(512)(128)(4,1)S(1)}, u32[]{:S(2)}) copy-start(pred[8]{0:T(512)(128)(4,1)S(1)} %get-tuple-element.319) | copy-start | bytes 28
  18.0 7.0 %copy-start = (f32[5,8,8,8,128]{4,3,2,1,0:T(8,128)S(1)}, f32[5,8,8,8,128]{4,3,2,1,0:T(8,128)}, u32[]{:S(2)}) copy-start(f32[5,8,8,8,128]{4,3,2,1,0:T(8,128)} %param.33) | copy-start | bytes 3932164
  23.3 48.6 %collective-permute-start = (f32[5,8,8,8]{2,1,0,3:T(8,128)}, f32[5,8,8,8]{2,1,0,3:T(8,128)}, u32[]{:S(2)}, u32[]{:S(2)}) collective-permute-start(f32[5,8,8,8]{2,1,0,3:T(8,128)} %select_bitcast_fusion.6), channel_id=1, source_target_pairs={{0,1},{1,0},{2,3},{3,2},{4,5},{5,4},{6,7},{7,6},{8,9},{9,8},{10,11... | collective-permute-start | bytes 30728 | tf_op jit(solution)/shard_map/ppermute | solution.py:32
  25.8 5.0 %copy-start.27 = (f32[1,8,8,1,128]{4,3,2,1,0:T(1,128)}, f32[1,8,8,1,128]{4,3,2,1,0:T(1,128)S(1)}, u32[]{:S(2)}) copy-start(f32[1,8,8,1,128]{4,3,2,1,0:T(1,128)S(1)} %get-tuple-element.220) | copy-start | bytes 98308
  25.8 5.6 %copy-start.18 = (f32[1,8,8,1,128]{4,3,2,1,0:T(1,128)}, f32[1,8,8,1,128]{4,3,2,1,0:T(1,128)S(1)}, u32[]{:S(2)}) copy-start(f32[1,8,8,1,128]{4,3,2,1,0:T(1,128)S(1)} %get-tuple-element.221) | copy-start | bytes 98308
  27.2 6.0 %copy-start.29 = (f32[1,8,1,8,128]{4,3,2,1,0:T(8,128)}, f32[1,8,1,8,128]{4,3,2,1,0:T(8,128)S(1)}, u32[]{:S(2)}) copy-start(f32[1,8,1,8,128]{4,3,2,1,0:T(8,128)S(1)} %get-tuple-element.227) | copy-start | bytes 98308
  27.2 6.6 %copy-start.20 = (f32[1,8,1,8,128]{4,3,2,1,0:T(8,128)}, f32[1,8,1,8,128]{4,3,2,1,0:T(8,128)S(1)}, u32[]{:S(2)}) copy-start(f32[1,8,1,8,128]{4,3,2,1,0:T(8,128)S(1)} %get-tuple-element.229) | copy-start | bytes 98308
  37.4 4.9 %copy-start.59 = (s32[1024]{0:T(1024)}, s32[1024]{0:T(1024)S(1)}, u32[]{:S(2)}) copy-start(s32[1024]{0:T(1024)S(1)} %get-tuple-element.323) | copy-start | bytes 12292
  57.5 4.6 %copy-start.40 = (f32[1,8,8,1,128]{4,3,2,1,0:T(1,128)S(1)}, f32[1,8,8,1,128]{4,3,2,1,0:T(1,128)}, u32[]{:S(2)}) copy-start(f32[1,8,8,1,128]{4,3,2,1,0:T(1,128)} %get-tuple-element.218) | copy-start | bytes 98308
  57.5 5.2 %copy-start.77 = (s32[128]{0:T(128)S(1)}, s32[128]{0:T(128)}, u32[]{:S(2)}) copy-start(s32[128]{0:T(128)} %get-tuple-element.301) | copy-start | bytes 1540
  57.5 5.2 %copy-start.78 = (s32[128]{0:T(128)S(1)}, s32[128]{0:T(128)}, u32[]{:S(2)}) copy-start(s32[128]{0:T(128)} %get-tuple-element.303) | copy-start | bytes 1540
  57.5 5.8 %copy-start.46 = (f32[1,8,1,8,128]{4,1,3,2,0:T(8,128)S(1)}, f32[1,8,1,8,128]{4,1,3,2,0:T(8,128)}, u32[]{:S(2)}) copy-start(f32[1,8,1,8,128]{4,1,3,2,0:T(8,128)} %copy.1598) | copy-start | bytes 98308
  57.5 5.8 %copy-start.39 = (f32[1,8,1,8,128]{4,3,2,1,0:T(8,128)S(1)}, f32[1,8,1,8,128]{4,3,2,1,0:T(8,128)}, u32[]{:S(2)}) copy-start(f32[1,8,1,8,128]{4,3,2,1,0:T(8,128)} %get-tuple-element.228) | copy-start | bytes 98308
  57.6 6.4 %copy-start.21 = (f32[1,8,1,8,128]{4,3,2,1,0:T(8,128)S(1)}, f32[1,8,1,8,128]{4,3,2,1,0:T(8,128)}, u32[]{:S(2)}) copy-start(f32[1,8,1,8,128]{4,3,2,1,0:T(8,128)} %copy-done.20) | copy-start | bytes 98308
  57.6 6.4 %copy-start.25 = (f32[1,8,1,8,128]{4,3,2,1,0:T(8,128)S(1)}, f32[1,8,1,8,128]{4,3,2,1,0:T(8,128)}, u32[]{:S(2)}) copy-start(f32[1,8,1,8,128]{4,3,2,1,0:T(8,128)} %get-tuple-element.226) | copy-start | bytes 98308
  60.1 4.5 %copy-start.38 = (f32[1,8,1,8,128]{4,3,2,1,0:T(8,128)S(1)}, f32[1,8,1,8,128]{4,3,2,1,0:T(8,128)}, u32[]{:S(2)}) copy-start(f32[1,8,1,8,128]{4,3,2,1,0:T(8,128)} %get-tuple-element.225) | copy-start | bytes 98308
  60.1 5.8 %copy-start.72 = (pred[128]{0:T(512)(128)(4,1)S(1)}, pred[128]{0:T(512)(128)(4,1)}, u32[]{:S(2)}) copy-start(pred[128]{0:T(512)(128)(4,1)} %get-tuple-element.306) | copy-start | bytes 388
  67.5 18.4 %copy-start.58 = (s32[1024]{0:T(1024)}, s32[1024]{0:T(1024)S(1)}, u32[]{:S(2)}) copy-start(s32[1024]{0:T(1024)S(1)} %pad_clamp_fusion.3) | copy-start | bytes 12292
  78.3 6.7 %collective-permute-start.1 = (f32[5,8,8,8]{2,1,0,3:T(8,128)S(1)}, f32[5,8,8,8]{2,1,0,3:T(8,128)}, u32[]{:S(2)}, u32[]{:S(2)}) collective-permute-start(f32[5,8,8,8]{2,1,0,3:T(8,128)S(1)} %select_bitcast_fusion.5), channel_id=1, source_target_pairs={{0,1},{1,0},{2,3},{3,2},{4,5},{5,4},{6,7},{7,6},{8,9},{9,8},{10,11... | collective-permute-start | bytes 30728 | tf_op jit(solution)/shard_map/ppermute | solution.py:32
  99.5 11.2 %collective-permute-start.3 = (f32[5,8,8,128]{3,1,2,0:T(8,128)S(1)}, f32[5,8,8,128]{3,1,2,0:T(8,128)S(1)}, u32[]{:S(2)}, u32[]{:S(2)}) collective-permute-start(f32[5,8,8,128]{3,1,2,0:T(8,128)S(1)} %get-tuple-element.169), channel_id=1, source_target_pairs={{0,2},{1,3},{2,4},{3,5},{4,6},{5,7},{6,8},{7,9},{8,10},{9,11},{10,... | collective-permute-start | bytes 491528 | tf_op jit(solution)/shard_map/ppermute | solution.py:37
  100.0 11.5 %copy-start.61 = (s32[1024]{0:T(1024)}, s32[1024]{0:T(1024)S(1)}, u32[]{:S(2)}) copy-start(s32[1024]{0:T(1024)S(1)} %pad_clamp_fusion) | copy-start | bytes 12292
  116.3 6.2 %copy-start.1 = (f32[5,8,8,8,128]{4,3,2,1,0:T(8,128)S(1)}, f32[5,8,8,8,128]{4,3,2,1,0:T(8,128)}, u32[]{:S(2)}) copy-start(f32[5,8,8,8,128]{4,3,2,1,0:T(8,128)} %param.33) | copy-start | bytes 3932164
  130.1 90.0 %collective-permute-start.6 = (f32[5,8,8,128]{3,1,0,2:T(8,128)}, f32[5,8,8,128]{3,1,0,2:T(8,128)}, u32[]{:S(2)}, u32[]{:S(2)}) collective-permute-start(f32[5,8,8,128]{3,1,0,2:T(8,128)} %slice_bitcast_fusion.6), channel_id=1, source_target_pairs={{0,254},{1,255},{2,0},{3,1},{4,2},{5,3},{6,4},{7,5},{8,6},{9,7},{1... | collective-permute-start | bytes 491528 | tf_op jit(solution)/shard_map/ppermute | solution.py:37
  132.9 7.8 %copy-start.6 = (f32[3,8,8,128]{3,1,2,0:T(8,128)}, f32[3,8,8,128]{3,1,2,0:T(8,128)S(1)}, u32[]{:S(2)}) copy-start(f32[3,8,8,128]{3,1,2,0:T(8,128)S(1)} %get-tuple-element.285) | copy-start | bytes 294916
  132.9 4.7 %copy-start.67 = (pred[8]{0:T(512)(128)(4,1)S(1)}, pred[8]{0:T(512)(128)(4,1)}, u32[]{:S(2)}) copy-start(pred[8]{0:T(512)(128)(4,1)} %copy-done.66) | copy-start | bytes 28
  138.3 49.4 %collective-permute-start.4 = (f32[5,8,8,8]{2,1,0,3:T(8,128)}, f32[5,8,8,8]{2,1,0,3:T(8,128)}, u32[]{:S(2)}, u32[]{:S(2)}) collective-permute-start(f32[5,8,8,8]{2,1,0,3:T(8,128)} %select_bitcast_fusion.2), channel_id=1, source_target_pairs={{0,1},{1,0},{2,3},{3,2},{4,5},{5,4},{6,7},{7,6},{8,9},{9,8},{10,11... | collective-permute-start | bytes 30728 | tf_op jit(solution)/shard_map/ppermute | solution.py:32
  195.8 4.7 %copy-start.65 = (pred[8]{0:T(512)(128)(4,1)S(1)}, pred[8]{0:T(512)(128)(4,1)}, u32[]{:S(2)}) copy-start(pred[8]{0:T(512)(128)(4,1)} %get-tuple-element.318) | copy-start | bytes 28
  200.5 10.2 %collective-permute-start.5 = (f32[5,8,8,8]{2,1,0,3:T(8,128)S(1)}, f32[5,8,8,8]{2,1,0,3:T(8,128)S(1)}, u32[]{:S(2)}, u32[]{:S(2)}) collective-permute-start(f32[5,8,8,8]{2,1,0,3:T(8,128)S(1)} %select_bitcast_fusion.1), channel_id=1, source_target_pairs={{0,1},{1,0},{2,3},{3,2},{4,5},{5,4},{6,7},{7,6},{8,9},{9,8},{10,11... | collective-permute-start | bytes 30728 | tf_op jit(solution)/shard_map/ppermute | solution.py:32
  231.8 10.8 %collective-permute-start.7 = (f32[5,8,8,128]{3,1,0,2:T(8,128)S(1)}, f32[5,8,8,128]{3,1,0,2:T(8,128)S(1)}, u32[]{:S(2)}, u32[]{:S(2)}) collective-permute-start(f32[5,8,8,128]{3,1,0,2:T(8,128)S(1)} %get-tuple-element.157), channel_id=1, source_target_pairs={{0,2},{1,3},{2,4},{3,5},{4,6},{5,7},{6,8},{7,9},{8,10},{9,11},{10,... | collective-permute-start | bytes 491528 | tf_op jit(solution)/shard_map/ppermute | solution.py:37
  (60 other events, 114.2 us)
where the time goes:
time: 263 us; the launch traced here: 259 us
  local copies, waits for them, and re-layouts  171 us (65%)
  other arithmetic  40.6 us (15%)
  starting transfers between devices  16.8 us (6%)
  matrix products  14.3 us (5%)
  waiting for transfers between devices  14 us (5%)
    gather x36, local copies, waits for them, and re-layouts, take_cols(): return jnp.take(table, columns, axis=-1)  90.3 us
    unnamed x188, local copies, waits for them, and re-layouts  14.7 us
    ppermute x4, starting transfers between devices, passed_along(): lax.ppermute(array, axis, [(i, (i + by) % devices) for i in range(devices)])  14.4 us
    dot_general x6, matrix products, volume_part(): jnp.einsum(FORMS[normal], deriv, fluxes, precision=lax.Precision.HIGHEST)  14.3 us
    ppermute x4, waiting for transfers between devices, passed_along(): lax.ppermute(array, axis, [(i, (i + by) % devices) for i in range(devices)])  13.9 us
    scatter-add x4, local copies, waits for them, and re-layouts, add_surface(): rate.at[lower_idx].add(lift * (lower_star[normal] - own_lower[normal]))  12 us
    scatter-add x6, local copies, waits for them, and re-layouts, add_surface(): rate.at[upper_idx].add(lift * (own_upper[normal] - upper_star[normal]))  10.4 us
    unnamed x43, other arithmetic  8.54 us
  transfers between devices with their start and end apart: 8, of which 2 were waited for; matrix products, arithmetic and copies ran while one was open for 63% of the time, Pallas kernels for 0%

commit v1 on v0

v1 whole, which is shorter than its diff:
```python
import functools

import jax
import jax.numpy as jnp
import numpy as np
from jax import lax
from jax.experimental import pallas as pl
from jax.experimental.pallas import tpu as pltpu
from jax.sharding import PartitionSpec as P

MESH = pl.DeviceIdType.MESH
GAMMA = 1.4
STEP = 0.003
NODES = 8
ELEMS = 128
LAST = NODES - 1
LIFT = LAST * (LAST + 1) / 2.0
LOBATTO_EIGHT = (
    -1.0,
    -0.8717401485096066,
    -0.5917001814331423,
    -0.2092992179024789,
    0.2092992179024789,
    0.5917001814331423,
    0.8717401485096066,
    1.0,
)


def folded_matrix():
    points = np.array(LOBATTO_EIGHT)
    identity = np.eye(NODES)
    spacing = points[:, None] - points[None, :] + identity
    weights = 1.0 / np.prod(spacing, axis=1)
    matrix = weights[None, :] / weights[:, None] / spacing
    matrix = matrix * (1.0 - identity)
    matrix = matrix - identity * np.sum(matrix, axis=1)[:, None]
    matrix = -matrix
    matrix[LAST, LAST] += LIFT
    matrix[0, 0] -= LIFT
    return matrix


MATRIX = folded_matrix()
EVEN = 0.5 * (MATRIX[:4, :4] + MATRIX[:4, :3:-1])
ODD = 0.5 * (MATRIX[:4, :4] - MATRIX[:4, :3:-1])


def derivative(values):
    even = [values[j] + values[LAST - j] for j in range(4)]
    odd = [values[j] - values[LAST - j] for j in range(4)]
    result = [None] * NODES
    for i in range(4):
        a = even[0] * float(EVEN[i, 0])
        b = odd[0] * float(ODD[i, 0])
        for j in range(1, 4):
            a = a + even[j] * float(EVEN[i, j])
            b = b + odd[j] * float(ODD[i, j])
        result[i] = b + a
        result[LAST - i] = b - a
    return result


def primitive(q):
    inverse = 1.0 / q[0]
    v = [q[1] * inverse, q[2] * inverse, q[3] * inverse]
    p = (GAMMA - 1.0) * (q[4] - 0.5 * (q[1] * v[0] + q[2] * v[1] + q[3] * v[2]))
    return inverse, v, p


def side(q, normal):
    inverse, v, p = primitive(q)
    speed = v[normal]
    flux = [q[1 + normal]]
    for column in range(3):
        term = q[1 + column] * speed
        flux.append(term + p if column == normal else term)
    flux.append((q[4] + p) * speed)
    wave = jnp.abs(speed) + jnp.sqrt(GAMMA * p * inverse)
    return flux, wave


def rusanov(left, right, normal):
    flux_left, wave_left = side(left, normal)
    flux_right, wave_right = side(right, normal)
    wave = jnp.maximum(wave_left, wave_right)
    return [
        0.5 * ((flux_left[c] + flux_right[c]) - wave * (right[c] - left[c])) for c in range(5)
    ]


def pick(table, columns):
    return jnp.take_along_axis(table, columns, axis=1, mode="promise_in_bounds")


def kernel(
    devices,
    state_hbm,
    neighbours_ref,
    out_hbm,
    u,
    r,
    prim,
    index,
    send_z,
    recv_z,
    recv_y,
    star_z,
    in_sem,
    out_sem,
    send_sem,
    recv_sem,
):
    me = lax.axis_index("dev")
    above = lax.rem(me + 2, devices)
    below = lax.rem(me + devices - 2, devices)
    partner = me + 1 - 2 * lax.rem(me, 2)

    load = pltpu.make_async_copy(state_hbm, u, in_sem)
    load.start()

    barrier = pltpu.get_barrier_semaphore()
    for other in (above, below, partner):
        pl.semaphore_signal(barrier, inc=1, device_id=(other,), device_id_type=MESH)

    ids = neighbours_ref[...]
    local = jnp.bitwise_and(ids, ELEMS - 1)
    remote = (jnp.right_shift(ids, 7) != me).astype(jnp.int32)
    for f in range(6):
        index[f] = jnp.broadcast_to(local[f : f + 1], (8, ELEMS))
    index[6] = jnp.broadcast_to(remote[2:3], (8, ELEMS))
    index[7] = jnp.broadcast_to(remote[3:4], (8, ELEMS))

    pl.semaphore_wait(barrier, 3)
    load.wait()

    def send(slot, source, target, device):
        copy = pltpu.make_async_remote_copy(
            src_ref=source,
            dst_ref=target,
            send_sem=send_sem.at[slot],
            recv_sem=recv_sem.at[slot],
            device_id=(device,),
            device_id_type=MESH,
        )
        copy.start()
        return copy

    def rows_j(j):
        return pl.ds(j * 8, 8)

    def rows_k(k):
        return pl.ds(k, 8, stride=8)

    def send_y(section):
        lower = send(4 + 2 * section, u.at[:, :, pl.ds(0, 8)], recv_y.at[2 * section], partner)
        upper = send(5 + 2 * section, u.at[:, :, pl.ds(56, 8)], recv_y.at[2 * section + 1], partner)
        return lower, upper

    def pack(i, carry):
        for c in range(5):
            send_z[0, c, i] = u[c, i, rows_k(0)]
            send_z[1, c, i] = u[c, i, rows_k(LAST)]
        return carry

    lax.fori_loop(0, 8, pack, 0)
    z_copies = [
        send(0, send_z.at[0], recv_z.at[0], below),
        send(1, send_z.at[1], recv_z.at[1], above),
    ]
    y_copies = [send_y(0)]

    def volume(section):
        def slab(i, carry):
            for j in range(8):
                q = [u[c, i, rows_j(j)] for c in range(5)]
                if section:
                    q = [q[c] + STEP * r[c, i, rows_j(j)] for c in range(5)]
                    for c in range(5):
                        u[c, i, rows_j(j)] = q[c]
                _, v, p = primitive(q)
                for d in range(3):
                    prim[d, i, rows_j(j)] = v[d]
                prim[3, i, rows_j(j)] = p
                prim[4, i, rows_j(j)] = q[4] + p
            return carry

        lax.fori_loop(0, 8, slab, 0)
        if section:
            y_copies.append(send_y(1))

        def fluxes(normal, at):
            speed = None
            for c in range(5):
                if c == 0:
                    yield c, [u[1 + normal, *at(n)] for n in range(8)]
                    continue
                if speed is None:
                    speed = [prim[normal, *at(n)] for n in range(8)]
                if c == 4:
                    yield c, [prim[4, *at(n)] * speed[n] for n in range(8)]
                    continue
                flux = [u[c, *at(n)] * speed[n] for n in range(8)]
                if c == 1 + normal:
                    flux = [flux[n] + prim[3, *at(n)] for n in range(8)]
                yield c, flux

        def along_j(i, carry):
            at = lambda n: (i, rows_j(n))
            for c, flux in fluxes(1, at):
                rate = derivative(flux)
                for n in range(8):
                    if section:
                        r[c, *at(n)] += rate[n]
                    else:
                        r[c, *at(n)] = rate[n]
            at_k = lambda n: (i, rows_k(n))
            for c, flux in fluxes(2, at_k):
                rate = derivative(flux)
                for n in range(8):
                    r[c, *at_k(n)] = r[c, *at_k(n)] + rate[n]
            return carry

        lax.fori_loop(0, 8, along_j, 0)

        def along_i(j, carry):
            rows = pl.ds(pl.multiple_of(j * 8, 8), 8)
            at = lambda n: (n, rows)
            for c, flux in fluxes(0, at):
                rate = derivative(flux)
                for n in range(8):
                    r[c, *at(n)] += rate[n]
            return carry

        lax.fori_loop(0, 8, along_i, 0)

    def surface_x():
        def face(j, carry):
            rows = pl.ds(pl.multiple_of(j * 8, 8), 8)
            left = [u[c, LAST, rows] for c in range(5)]
            right = [pick(u[c, 0, rows], index[1]) for c in range(5)]
            star = rusanov(left, right, 0)
            for c in range(5):
                lifted = LIFT * star[c]
                r[c, LAST, rows] -= lifted
                r[c, 0, rows] += pick(lifted, index[0])
            return carry

        lax.fori_loop(0, 8, face, 0)

    def surface_y(section):
        for copy in y_copies[section]:
            copy.wait_recv()
        got_lower = recv_y.at[2 * section]
        got_upper = recv_y.at[2 * section + 1]

        def face(i, carry):
            lower = [u[c, i, rows_j(0)] for c in range(5)]
            upper = [u[c, i, rows_j(LAST)] for c in range(5)]
            remote_low = index[6] != 0
            remote_up = index[7] != 0
            right = [
                jnp.where(remote_up, pick(got_lower[c, i], index[3]), pick(lower[c], index[3]))
                for c in range(5)
            ]
            star = rusanov(upper, right, 1)
            for c in range(5):
                r[c, i, rows_j(LAST)] -= LIFT * star[c]
            left = [
                jnp.where(remote_low, pick(got_upper[c, i], index[2]), pick(upper[c], index[2]))
                for c in range(5)
            ]
            star = rusanov(left, lower, 1)
            for c in range(5):
                r[c, i, rows_j(0)] += LIFT * star[c]
            return carry

        lax.fori_loop(0, 8, face, 0)

    def surface_z(section):
        def face(i, carry):
            left = [u[c, i, rows_k(LAST)] for c in range(5)]
            right = [pick(recv_z[2 * section, c, i], index[5]) for c in range(5)]
            if section:
                right = [right[c] + STEP * star_z[0, c, i] for c in range(5)]
            star = rusanov(left, right, 2)
            for c in range(5):
                lifted = LIFT * star[c]
                r[c, i, rows_k(LAST)] = r[c, i, rows_k(LAST)] - lifted
                if not section:
                    star_z[0, c, i] = lifted
            left = [pick(recv_z[2 * section + 1, c, i], index[4]) for c in range(5)]
            if section:
                left = [left[c] - STEP * star_z[1, c, i] for c in range(5)]
            right = [u[c, i, rows_k(0)] for c in range(5)]
            star = rusanov(left, right, 2)
            for c in range(5):
                lifted = LIFT * star[c]
                r[c, i, rows_k(0)] = r[c, i, rows_k(0)] + lifted
                if not section:
                    star_z[1, c, i] = lifted
            if section:
                for c in range(5):
                    r[c, i] = (0.5 * STEP) * r[c, i]
            return carry

        lax.fori_loop(0, 8, face, 0)

    volume(0)
    surface_x()
    surface_y(0)

    def pack_again(i, carry):
        for c in range(5):
            for s, k in ((0, 0), (1, LAST)):
                send_z[2 + s, c, i] = u[c, i, rows_k(k)] + STEP * r[c, i, rows_k(k)]
        return carry

    lax.fori_loop(0, 8, pack_again, 0)
    z_copies += [
        send(2, send_z.at[2], recv_z.at[2], below),
        send(3, send_z.at[3], recv_z.at[3], above),
    ]
    for copy in z_copies[:2]:
        copy.wait_recv()
    surface_z(0)
    for copy in y_copies[0]:
        copy.wait_send()

    volume(1)
    surface_x()
    surface_y(1)
    for copy in z_copies[2:]:
        copy.wait_recv()
    surface_z(1)

    store = pltpu.make_async_copy(r, out_hbm, out_sem)
    store.start()
    for copy in z_copies:
        copy.wait_send()
    for copy in y_copies[1]:
        copy.wait_send()
    store.wait()


def body(devices, state, neighbours):
    flat = state.reshape(5, 8, 64, ELEMS)
    change = pl.pallas_call(
        functools.partial(kernel, devices),
        out_shape=jax.ShapeDtypeStruct(flat.shape, jnp.float32),
        in_specs=[pl.BlockSpec(memory_space=pl.ANY), pl.BlockSpec(memory_space=pltpu.VMEM)],
        out_specs=pl.BlockSpec(memory_space=pl.ANY),
        scratch_shapes=[
            pltpu.VMEM((5, 8, 64, ELEMS), jnp.float32),
            pltpu.VMEM((5, 8, 64, ELEMS), jnp.float32),
            pltpu.VMEM((5, 8, 64, ELEMS), jnp.float32),
            pltpu.VMEM((8, 8, ELEMS), jnp.int32),
            pltpu.VMEM((4, 5, 8, 8, ELEMS), jnp.float32),
            pltpu.VMEM((4, 5, 8, 8, ELEMS), jnp.float32),
            pltpu.VMEM((4, 5, 8, 8, ELEMS), jnp.float32),
            pltpu.VMEM((2, 5, 8, 8, ELEMS), jnp.float32),
            pltpu.SemaphoreType.DMA,
            pltpu.SemaphoreType.DMA,
            pltpu.SemaphoreType.DMA((8,)),
            pltpu.SemaphoreType.DMA((8,)),
        ],
        compiler_params=pltpu.CompilerParams(
            collective_id=0, has_side_effects=True, vmem_limit_bytes=40 * 1024 * 1024
        ),
        cost_estimate=pl.CostEstimate(
            flops=25_000_000, bytes_accessed=2_700_000, transcendentals=0
        ),
    )(flat, neighbours)
    return change.reshape(state.shape)


def solution(mesh):
    devices = mesh.shape["dev"]
    in_specs = (P(None, None, None, None, "dev"), P(None, "dev"))
    out_specs = P(None, None, None, None, "dev")
    return jax.shard_map(
        functools.partial(body, devices),
        mesh=mesh,
        in_specs=in_specs,
        out_specs=out_specs,
        check_vma=False,
    )
```

time: 263 us -> 26 us (0.10); the launches traced: 259 us -> 25.9 us
  local copies, waits for them, and re-layouts: 171 us -> 3.06 us
  other arithmetic: 40.6 us -> 0 us
  Pallas kernels: 0 us -> 22.8 us
  starting transfers between devices: 16.8 us -> 0 us
  matrix products: 14.3 us -> 0 us
  waiting for transfers between devices: 14 us -> 0 us
    gather x36 -> x0, local copies, waits for them, and re-layouts: 90.3 us -> none  [take_cols(): return jnp.take(table, columns, axis=-1)]
    pallas_call x0 -> x1, Pallas kernels: none -> 22.8 us  [body(): pl.pallas_call(functools.partial(kernel, devices), out_shape=jax.ShapeDty...]
    scatter-add x10 -> x0, local copies, waits for them, and re-layouts: 22.4 us -> none  [the longest x4 12 us: add_surface(): rate.at[lower_idx].add(lift * (lower_star[normal] - own_lower[normal]))]
    ppermute x8 -> x0, starting transfers between devices: 16.8 us -> none  [the longest x4 14.4 us: passed_along(): lax.ppermute(array, axis, [(i, (i + by) % devices) for i in range(devices)])]
    dot_general x6 -> x0, matrix products: 14.3 us -> none  [volume_part(): jnp.einsum(FORMS[normal], deriv, fluxes, precision=lax.Precision.HIGHEST)]
    ppermute x8 -> x0, waiting for transfers between devices: 14 us -> none  [the longest x4 13.9 us: passed_along(): lax.ppermute(array, axis, [(i, (i + by) % devices) for i in range(devices)])]
    slice x17 -> x0, local copies, waits for them, and re-layouts: 13.1 us -> none  [the longest x6 7.15 us: face(): lax.index_in_dim(field, sided * (field.shape[1] - 1), 1 + normal, keepdim...]
    unnamed x188 -> x5, local copies, waits for them, and re-layouts: 14.7 us -> 3.06 us
  transfers between devices with their start and end apart: 8 -> 0, of which waited for: 2 -> 0; matrix products, arithmetic and copies ran while one was open for 63% -> 0% of each run, Pallas kernels for 0% -> 0%
where the time goes in v1:
time: 26 us; the launch traced here: 25.9 us
  Pallas kernels  22.8 us (88%)
  local copies, waits for them, and re-layouts  3.06 us (12%)
    pallas_call x1, Pallas kernels, body(): pl.pallas_call(functools.partial(kernel, devices), out_shape=jax.ShapeDty...  22.8 us
    unnamed x5, local copies, waits for them, and re-layouts  3.06 us

profile of v1, /device:TPU:1, one launch (start us, length us, event | category | flops | bytes accessed | tf_op | source)
XLA Modules:
  0.0 25.9 jit_solution(12081827143448815409)
XLA Ops:
  0.0 0.0 copy-start
  0.0 1.3 %copy-done = f32[5,8,8,8,128]{4,3,2,1,0:T(8,128)S(1)} copy-done((f32[5,8,8,8,128]{4,3,2,1,0:T(8,128)S(1)}, f32[5,8,8,8,128]{4,3,2,1,0:T(8,128)}, u32[]{:S(2)}) %copy-start) | copy-done | bytes 1310744
  1.3 0.0 copy-start.1
  1.3 0.7 %copy-done.1 = s32[6,128]{1,0:T(8,128)S(1)} copy-done((s32[6,128]{1,0:T(8,128)S(1)}, s32[6,128]{1,0:T(8,128)}, u32[]{:S(2)}) %copy-start.1) | copy-done | bytes 3096
  2.0 22.8 %shard_map.28 = f32[5,8,64,128]{3,2,1,0:T(8,128)S(1)} custom-call(f32[5,8,64,128]{3,2,1,0:T(8,128)S(1)} %bitcast.3, s32[6,128]{1,0:T(8,128)S(1)} %copy-done.1), custom_call_target="tpu_custom_call" | custom-call | flops 25000000 | bytes 2700000 | tf_op jit(solution)/shard_map/pallas_call | solution.py:348
  24.8 1.1 %copy.4 = f32[5,8,8,8,128]{4,3,2,1,0:T(8,128)} copy(f32[5,8,8,8,128]{4,3,2,1,0:T(8,128)S(1)} %bitcast.2) | data formatting | bytes 2621440
Async XLA Ops:
  0.0 1.3 %copy-start = (f32[5,8,8,8,128]{4,3,2,1,0:T(8,128)S(1)}, f32[5,8,8,8,128]{4,3,2,1,0:T(8,128)}, u32[]{:S(2)}) copy-start(f32[5,8,8,8,128]{4,3,2,1,0:T(8,128)} %param.2) | copy-start | bytes 3932164
  1.3 0.7 %copy-start.1 = (s32[6,128]{1,0:T(8,128)S(1)}, s32[6,128]{1,0:T(8,128)}, u32[]{:S(2)}) copy-start(s32[6,128]{1,0:T(8,128)} %neighbours_ref.1) | copy-start | bytes 9220

commit v2 on v1

--- a/solution.py
+++ b/solution.py
@@ -96,18 +96,17 @@
 def kernel(
     devices,
     state_hbm,
-    neighbours_ref,
-    out_hbm,
+    neighbours_hbm,
+    r,
     u,
-    r,
     prim,
+    ids_ref,
     index,
     send_z,
     recv_z,
     recv_y,
     star_z,
     in_sem,
-    out_sem,
     send_sem,
     recv_sem,
 ):
@@ -116,14 +115,20 @@
     below = lax.rem(me + devices - 2, devices)
     partner = me + 1 - 2 * lax.rem(me, 2)
 
-    load = pltpu.make_async_copy(state_hbm, u, in_sem)
-    load.start()
+    loads = [
+        pltpu.make_async_copy(state_hbm.at[:, i], u.at[:, i], in_sem.at[i]) for i in range(8)
+    ]
+    for load in loads:
+        load.start()
+    load_ids = pltpu.make_async_copy(neighbours_hbm, ids_ref, in_sem.at[8])
+    load_ids.start()
 
     barrier = pltpu.get_barrier_semaphore()
     for other in (above, below, partner):
         pl.semaphore_signal(barrier, inc=1, device_id=(other,), device_id_type=MESH)
 
-    ids = neighbours_ref[...]
+    load_ids.wait()
+    ids = ids_ref[...]
     local = jnp.bitwise_and(ids, ELEMS - 1)
     remote = (jnp.right_shift(ids, 7) != me).astype(jnp.int32)
     for f in range(6):
@@ -131,8 +136,6 @@
     index[6] = jnp.broadcast_to(remote[2:3], (8, ELEMS))
     index[7] = jnp.broadcast_to(remote[3:4], (8, ELEMS))
 
-    pl.semaphore_wait(barrier, 3)
-    load.wait()
 
     def send(slot, source, target, device):
         copy = pltpu.make_async_remote_copy(
@@ -157,13 +160,12 @@
         upper = send(5 + 2 * section, u.at[:, :, pl.ds(56, 8)], recv_y.at[2 * section + 1], partner)
         return lower, upper
 
-    def pack(i, carry):
+    for i in range(8):
+        loads[i].wait()
         for c in range(5):
             send_z[0, c, i] = u[c, i, rows_k(0)]
             send_z[1, c, i] = u[c, i, rows_k(LAST)]
-        return carry
-
-    lax.fori_loop(0, 8, pack, 0)
+    pl.semaphore_wait(barrier, 3)
     z_copies = [
         send(0, send_z.at[0], recv_z.at[0], below),
         send(1, send_z.at[1], recv_z.at[1], above),
@@ -246,7 +248,7 @@
                 r[c, 0, rows] += pick(lifted, index[0])
             return carry
 
-        lax.fori_loop(0, 8, face, 0)
+        lax.fori_loop(0, 8, face, 0, unroll=8)
 
     def surface_y(section):
         for copy in y_copies[section]:
@@ -275,7 +277,7 @@
                 r[c, i, rows_j(0)] += LIFT * star[c]
             return carry
 
-        lax.fori_loop(0, 8, face, 0)
+        lax.fori_loop(0, 8, face, 0, unroll=8)
 
     def surface_z(section):
         def face(i, carry):
@@ -304,7 +306,7 @@
                     r[c, i] = (0.5 * STEP) * r[c, i]
             return carry
 
-        lax.fori_loop(0, 8, face, 0)
+        lax.fori_loop(0, 8, face, 0, unroll=8)
 
     volume(0)
     surface_x()
@@ -316,7 +318,7 @@
                 send_z[2 + s, c, i] = u[c, i, rows_k(k)] + STEP * r[c, i, rows_k(k)]
         return carry
 
-    lax.fori_loop(0, 8, pack_again, 0)
+    lax.fori_loop(0, 8, pack_again, 0, unroll=8)
     z_copies += [
         send(2, send_z.at[2], recv_z.at[2], below),
         send(3, send_z.at[3], recv_z.at[3], above),
@@ -334,33 +336,29 @@
         copy.wait_recv()
     surface_z(1)
 
-    store = pltpu.make_async_copy(r, out_hbm, out_sem)
-    store.start()
     for copy in z_copies:
         copy.wait_send()
     for copy in y_copies[1]:
         copy.wait_send()
-    store.wait()
 
 
 def body(devices, state, neighbours):
     flat = state.reshape(5, 8, 64, ELEMS)
     change = pl.pallas_call(
         functools.partial(kernel, devices),
-        out_shape=jax.ShapeDtypeStruct(flat.shape, jnp.float32),
-        in_specs=[pl.BlockSpec(memory_space=pl.ANY), pl.BlockSpec(memory_space=pltpu.VMEM)],
-        out_specs=pl.BlockSpec(memory_space=pl.ANY),
+        out_shape=pltpu.VMEM(flat.shape, jnp.float32),
+        in_specs=[pl.BlockSpec(memory_space=pltpu.HBM), pl.BlockSpec(memory_space=pltpu.HBM)],
+        out_specs=pl.BlockSpec(memory_space=pltpu.VMEM),
         scratch_shapes=[
             pltpu.VMEM((5, 8, 64, ELEMS), jnp.float32),
             pltpu.VMEM((5, 8, 64, ELEMS), jnp.float32),
-            pltpu.VMEM((5, 8, 64, ELEMS), jnp.float32),
+            pltpu.VMEM((6, ELEMS), jnp.int32),
             pltpu.VMEM((8, 8, ELEMS), jnp.int32),
             pltpu.VMEM((4, 5, 8, 8, ELEMS), jnp.float32),
             pltpu.VMEM((4, 5, 8, 8, ELEMS), jnp.float32),
             pltpu.VMEM((4, 5, 8, 8, ELEMS), jnp.float32),
             pltpu.VMEM((2, 5, 8, 8, ELEMS), jnp.float32),
-            pltpu.SemaphoreType.DMA,
-            pltpu.SemaphoreType.DMA,
+            pltpu.SemaphoreType.DMA((9,)),
             pltpu.SemaphoreType.DMA((8,)),
             pltpu.SemaphoreType.DMA((8,)),
         ],
@@ -370,7 +368,10 @@
         cost_estimate=pl.CostEstimate(
             flops=25_000_000, bytes_accessed=2_700_000, transcendentals=0
         ),
-    )(flat, neighbours)
+    )(
+        pltpu.with_memory_space_constraint(flat, pltpu.HBM),
+        pltpu.with_memory_space_constraint(neighbours, pltpu.HBM),
+    )
     return change.reshape(state.shape)
 
 

time: 26 us -> 22.3 us (0.86)
  local copies, waits for them, and re-layouts: 3.06 us -> 1.06 us
  Pallas kernels: 22.8 us -> 21.1 us
    unnamed x5 -> x1, local copies, waits for them, and re-layouts: 3.06 us -> 1.06 us
    pallas_call x1, Pallas kernels: 22.8 us -> 21.1 us  [body(): pl.pallas_call(functools.partial(kernel, devices), out_shape=pltpu.VMEM(f...]
where the time goes in v2:
time: 22.3 us; the launch traced here: 22.2 us
  Pallas kernels  21.1 us (95%)
  local copies, waits for them, and re-layouts  1.06 us (5%)
    pallas_call x1, Pallas kernels, body(): pl.pallas_call(functools.partial(kernel, devices), out_shape=pltpu.VMEM(f...  21.1 us
    unnamed x1, local copies, waits for them, and re-layouts  1.06 us

profile of v2, /device:TPU:1, one launch (start us, length us, event | category | flops | bytes accessed | tf_op | source)
XLA Modules:
  0.0 22.2 jit_solution(15534911623625073502)
XLA Ops:
  0.0 21.1 %shard_map.28 = f32[5,8,64,128]{3,2,1,0:T(8,128)S(1)} custom-call(f32[5,8,64,128]{3,2,1,0:T(8,128)} %bitcast.3, s32[6,128]{1,0:T(8,128)} %neighbours_hbm.1), custom_call_target="tpu_custom_call" | custom-call | flops 25000000 | bytes 2700000 | tf_op jit(solution)/shard_map/pallas_call | solution.py:347
  21.1 1.1 %copy.4 = f32[5,8,8,8,128]{4,3,2,1,0:T(8,128)} copy(f32[5,8,8,8,128]{4,3,2,1,0:T(8,128)S(1)} %bitcast.2) | data formatting | bytes 2621440

commit v3 on v2

v3 whole, which is shorter than its diff:
```python
import functools

import jax
import jax.numpy as jnp
import numpy as np
from jax import lax
from jax.experimental import pallas as pl
from jax.experimental.pallas import tpu as pltpu
from jax.sharding import PartitionSpec as P

MESH = pl.DeviceIdType.MESH
GAMMA = 1.4
STEP = 0.003
NODES = 8
ELEMS = 128
LAST = NODES - 1
LIFT = LAST * (LAST + 1) / 2.0
ENDS = (0, LAST)
MIDDLE = tuple(range(1, LAST))
LOBATTO_EIGHT = (
    -1.0,
    -0.8717401485096066,
    -0.5917001814331423,
    -0.2092992179024789,
    0.2092992179024789,
    0.5917001814331423,
    0.8717401485096066,
    1.0,
)


def folded_matrix():
    points = np.array(LOBATTO_EIGHT)
    identity = np.eye(NODES)
    spacing = points[:, None] - points[None, :] + identity
    weights = 1.0 / np.prod(spacing, axis=1)
    matrix = weights[None, :] / weights[:, None] / spacing
    matrix = matrix * (1.0 - identity)
    matrix = matrix - identity * np.sum(matrix, axis=1)[:, None]
    matrix = -matrix
    matrix[LAST, LAST] += LIFT
    matrix[0, 0] -= LIFT
    return matrix


MATRIX = folded_matrix()
EVEN = 0.5 * (MATRIX[:4, :4] + MATRIX[:4, :3:-1])
ODD = 0.5 * (MATRIX[:4, :4] - MATRIX[:4, :3:-1])


def derivative(values, pairs=(0, 1, 2, 3)):
    even = {j: values[j] + values[LAST - j] for j in pairs}
    odd = {j: values[j] - values[LAST - j] for j in pairs}
    result = [None] * NODES
    for i in range(4):
        a = b = None
        for j in pairs:
            x = even[j] * float(EVEN[i, j])
            y = odd[j] * float(ODD[i, j])
            a = x if a is None else a + x
            b = y if b is None else b + y
        result[i] = b + a
        result[LAST - i] = b - a
    return result


def primitive(q):
    inverse = 1.0 / q[0]
    v = [q[1] * inverse, q[2] * inverse, q[3] * inverse]
    p = (GAMMA - 1.0) * (q[4] - 0.5 * (q[1] * v[0] + q[2] * v[1] + q[3] * v[2]))
    return inverse, v, p


def side(q, normal):
    inverse, v, p = primitive(q)
    speed = v[normal]
    flux = [q[1 + normal]]
    for column in range(3):
        term = q[1 + column] * speed
        flux.append(term + p if column == normal else term)
    flux.append((q[4] + p) * speed)
    wave = jnp.abs(speed) + jnp.sqrt(GAMMA * p * inverse)
    return flux, wave


def rusanov(left, right, normal):
    flux_left, wave_left = side(left, normal)
    flux_right, wave_right = side(right, normal)
    wave = jnp.maximum(wave_left, wave_right)
    return [
        0.5 * ((flux_left[c] + flux_right[c]) - wave * (right[c] - left[c])) for c in range(5)
    ]


def pick(table, columns):
    return jnp.take_along_axis(table, columns, axis=1, mode="promise_in_bounds")


def kernel(
    devices,
    state_hbm,
    neighbours_hbm,
    out,
    planes,
    r,
    prim,
    ids_ref,
    index,
    ends,
    recv_z,
    star_z,
    own_y_ends,
    own_y_middle,
    recv_y_ends,
    recv_y_middle,
    in_sem,
    send_sem,
    recv_sem,
):
    u = planes.reshape(5, 8, 64, ELEMS)
    me = lax.axis_index("dev")
    above = lax.rem(me + 2, devices)
    below = lax.rem(me + devices - 2, devices)
    partner = me + 1 - 2 * lax.rem(me, 2)

    loads = {
        k: pltpu.make_async_copy(state_hbm.at[:, :, :, k, :], planes.at[:, k], in_sem.at[k])
        for k in ENDS + MIDDLE
    }
    for load in loads.values():
        load.start()
    load_ids = pltpu.make_async_copy(neighbours_hbm, ids_ref, in_sem.at[8])
    load_ids.start()

    barrier = pltpu.get_barrier_semaphore()
    for other in (above, below, partner):
        pl.semaphore_signal(barrier, inc=1, device_id=(other,), device_id_type=MESH)

    def send(slot, source, target, device):
        copy = pltpu.make_async_remote_copy(
            src_ref=source,
            dst_ref=target,
            send_sem=send_sem.at[slot],
            recv_sem=recv_sem.at[slot],
            device_id=(device,),
            device_id_type=MESH,
        )
        copy.start()
        return copy

    def rows_i(i):
        if isinstance(i, int):
            return pl.ds(i * 8, 8)
        return pl.ds(pl.multiple_of(i * 8, 8), 8)

    def rows_j(j):
        return pl.ds(j, 8, stride=8)

    def rows_k(k):
        return pl.ds(k, 8, stride=8)

    def send_y(section, which):
        own, got, which_planes, slot = (
            (own_y_ends, recv_y_ends, ENDS, 4 + section)
            if which == ENDS
            else (own_y_middle, recv_y_middle, MIDDLE, 6 + section)
        )
        for n, k in enumerate(which_planes):
            for c in range(5):
                for side_y, j in ((0, 0), (1, LAST)):
                    own[section, side_y, c, n] = u[c, k, rows_j(j)]
        return send(slot, own.at[section], got.at[section], partner)

    def primitives(k, update):
        for i in range(8):
            q = [u[c, k, rows_i(i)] for c in range(5)]
            if update:
                q = [q[c] + STEP * r[c, k, rows_i(i)] for c in range(5)]
                for c in range(5):
                    u[c, k, rows_i(i)] = q[c]
            _, v, p = primitive(q)
            for d in range(3):
                prim[d, k, rows_i(i)] = v[d]
            prim[3, k, rows_i(i)] = p
            prim[4, k, rows_i(i)] = q[4] + p

    def fluxes(normal, at, nodes=tuple(range(8))):
        speed = {n: prim[normal, *at(n)] for n in nodes}
        for c in range(5):
            if c == 0:
                yield c, {n: u[1 + normal, *at(n)] for n in nodes}
                continue
            if c == 4:
                yield c, {n: prim[4, *at(n)] * speed[n] for n in nodes}
                continue
            flux = {n: u[c, *at(n)] * speed[n] for n in nodes}
            if c == 1 + normal:
                flux = {n: flux[n] + prim[3, *at(n)] for n in nodes}
            yield c, flux

    def in_plane(k):
        for normal, rows in ((0, rows_i), (1, rows_j)):
            at = lambda n: (k, rows(n))
            for c, flux in fluxes(normal, at):
                rate = derivative(flux)
                for n in range(8):
                    r[c, *at(n)] = r[c, *at(n)] + rate[n]

    def surface_x(k):
        left = [u[c, k, rows_i(LAST)] for c in range(5)]
        right = [pick(u[c, k, rows_i(0)], index[1]) for c in range(5)]
        star = rusanov(left, right, 0)
        for c in range(5):
            lifted = LIFT * star[c]
            r[c, k, rows_i(LAST)] -= lifted
            r[c, k, rows_i(0)] += pick(lifted, index[0])

    def surface_y(section, which):
        own, got, which_planes = (
            (own_y_ends, recv_y_ends, ENDS)
            if which == ENDS
            else (own_y_middle, recv_y_middle, MIDDLE)
        )
        for n, k in enumerate(which_planes):
            lower = [own[section, 0, c, n] for c in range(5)]
            upper = [own[section, 1, c, n] for c in range(5)]
            remote_low = index[6] != 0
            remote_up = index[7] != 0
            right = [
                jnp.where(
                    remote_up, pick(got[section, 0, c, n], index[3]), pick(lower[c], index[3])
                )
                for c in range(5)
            ]
            star = rusanov(upper, right, 1)
            for c in range(5):
                r[c, k, rows_j(LAST)] = r[c, k, rows_j(LAST)] - LIFT * star[c]
            left = [
                jnp.where(
                    remote_low, pick(got[section, 1, c, n], index[2]), pick(upper[c], index[2])
                )
                for c in range(5)
            ]
            star = rusanov(left, lower, 1)
            for c in range(5):
                r[c, k, rows_j(0)] = r[c, k, rows_j(0)] + LIFT * star[c]

    def loop(first, last, step, unroll=1):
        def wrapped(n, carry):
            step(n)
            return carry

        lax.fori_loop(first, last, wrapped, 0, unroll=unroll)

    for k in ENDS:
        loads[k].wait()
    pl.semaphore_wait(barrier, 3)
    z_copies = [
        send(0, planes.at[:, 0], recv_z.at[0], below),
        send(1, planes.at[:, LAST], recv_z.at[1], above),
    ]
    y_copies = [send_y(0, ENDS)]

    load_ids.wait()
    ids = ids_ref[...]
    local = jnp.bitwise_and(ids, ELEMS - 1)
    remote = (jnp.right_shift(ids, 7) != me).astype(jnp.int32)
    for f in range(6):
        index[f] = jnp.broadcast_to(local[f : f + 1], (8, ELEMS))
    index[6] = jnp.broadcast_to(remote[2:3], (8, ELEMS))
    index[7] = jnp.broadcast_to(remote[3:4], (8, ELEMS))

    for k in MIDDLE:
        loads[k].wait()
    y_copies.append(send_y(0, MIDDLE))

    loop(0, 8, lambda k: primitives(k, False))

    def along_k_first(i):
        at = lambda n: (n, rows_i(i))
        for c, flux in fluxes(2, at):
            rate = derivative(flux)
            for n in range(8):
                r[c, *at(n)] = rate[n]

    loop(0, 8, along_k_first)
    for k in ENDS:
        in_plane(k)
        surface_x(k)
    y_copies[0].wait_recv()
    surface_y(0, ENDS)

    for s, k in enumerate(ENDS):
        for i in range(8):
            for c in range(5):
                ends[s, c, i] = u[c, k, rows_i(i)] + STEP * r[c, k, rows_i(i)]
    z_copies += [
        send(2, ends.at[0], recv_z.at[2], below),
        send(3, ends.at[1], recv_z.at[3], above),
    ]

    loop(1, LAST, in_plane)
    loop(1, LAST, surface_x, 6)
    y_copies[1].wait_recv()
    surface_y(0, MIDDLE)

    loop(1, LAST, lambda k: primitives(k, True))
    y_copies.append(send_y(1, MIDDLE))
    loop(1, LAST, in_plane)

    def along_k_middle(i):
        at = lambda n: (n, rows_i(i))
        for c, flux in fluxes(2, at, MIDDLE):
            rate = derivative(flux, (1, 2, 3))
            for n in range(8):
                r[c, *at(n)] += rate[n]

    loop(0, 8, along_k_middle)
    loop(1, LAST, surface_x, 6)
    y_copies[2].wait_recv()
    surface_y(1, MIDDLE)

    for copy in z_copies[:2]:
        copy.wait()

    def surface_z_first(i):
        rows = rows_i(i)
        right = [pick(recv_z[0, c, i], index[5]) for c in range(5)]
        star = rusanov([u[c, LAST, rows] for c in range(5)], right, 2)
        for c in range(5):
            lifted = LIFT * star[c]
            star_z[0, c, i] = lifted
            r[c, LAST, rows] -= lifted
            u[c, LAST, rows] = ends[1, c, i] - STEP * lifted
        left = [pick(recv_z[1, c, i], index[4]) for c in range(5)]
        star = rusanov(left, [u[c, 0, rows] for c in range(5)], 2)
        for c in range(5):
            lifted = LIFT * star[c]
            star_z[1, c, i] = lifted
            r[c, 0, rows] += lifted
            u[c, 0, rows] = ends[0, c, i] + STEP * lifted

    loop(0, 8, surface_z_first, 8)
    y_copies.append(send_y(1, ENDS))
    for k in ENDS:
        primitives(k, False)
    for k in ENDS:
        in_plane(k)
        surface_x(k)

    def along_k_ends(i):
        at = lambda n: (n, rows_i(i))
        for c, flux in fluxes(2, at, ENDS):
            rate = derivative(flux, (0,))
            for n in ENDS:
                r[c, *at(n)] += rate[n]
            for n in MIDDLE:
                out[c, i, rows_k(n)] = (0.5 * STEP) * (r[c, *at(n)] + rate[n])

    loop(0, 8, along_k_ends)
    y_copies[3].wait_recv()
    surface_y(1, ENDS)

    for copy in z_copies[2:]:
        copy.wait_recv()

    def surface_z_second(i):
        rows = rows_i(i)
        right = [pick(recv_z[2, c, i], index[5]) + STEP * star_z[0, c, i] for c in range(5)]
        star = rusanov([u[c, LAST, rows] for c in range(5)], right, 2)
        for c in range(5):
            out[c, i, rows_k(LAST)] = (0.5 * STEP) * (r[c, LAST, rows] - LIFT * star[c])
        left = [pick(recv_z[3, c, i], index[4]) - STEP * star_z[1, c, i] for c in range(5)]
        star = rusanov(left, [u[c, 0, rows] for c in range(5)], 2)
        for c in range(5):
            out[c, i, rows_k(0)] = (0.5 * STEP) * (r[c, 0, rows] + LIFT * star[c])

    loop(0, 8, surface_z_second, 8)
    for copy in z_copies[2:]:
        copy.wait_send()
    for copy in y_copies:
        copy.wait_send()


def body(devices, state, neighbours):
    field = pltpu.VMEM((5, 8, 64, ELEMS), jnp.float32)
    faces = (5, 8, 8, ELEMS)
    change = pl.pallas_call(
        functools.partial(kernel, devices),
        out_shape=pltpu.VMEM((5, 8, 64, ELEMS), jnp.float32),
        in_specs=[pl.BlockSpec(memory_space=pltpu.HBM), pl.BlockSpec(memory_space=pltpu.HBM)],
        out_specs=pl.BlockSpec(memory_space=pltpu.VMEM),
        scratch_shapes=[
            pltpu.VMEM((5, 8, 8, 8, ELEMS), jnp.float32),
            field,
            field,
            pltpu.VMEM((6, ELEMS), jnp.int32),
            pltpu.VMEM((8, 8, ELEMS), jnp.int32),
            pltpu.VMEM((2,) + faces, jnp.float32),
            pltpu.VMEM((4,) + faces, jnp.float32),
            pltpu.VMEM((2,) + faces, jnp.float32),
            pltpu.VMEM((2, 2, 5, 2, 8, ELEMS), jnp.float32),
            pltpu.VMEM((2, 2, 5, 6, 8, ELEMS), jnp.float32),
            pltpu.VMEM((2, 2, 5, 2, 8, ELEMS), jnp.float32),
            pltpu.VMEM((2, 2, 5, 6, 8, ELEMS), jnp.float32),
            pltpu.SemaphoreType.DMA((9,)),
            pltpu.SemaphoreType.DMA((8,)),
            pltpu.SemaphoreType.DMA((8,)),
        ],
        compiler_params=pltpu.CompilerParams(
            collective_id=0, has_side_effects=True, vmem_limit_bytes=40 * 1024 * 1024
        ),
        cost_estimate=pl.CostEstimate(
            flops=25_000_000, bytes_accessed=2_700_000, transcendentals=0
        ),
    )(
        pltpu.with_memory_space_constraint(state, pltpu.HBM),
        pltpu.with_memory_space_constraint(neighbours, pltpu.HBM),
    )
    return change.reshape(state.shape)


def solution(mesh):
    devices = mesh.shape["dev"]
    in_specs = (P(None, None, None, None, "dev"), P(None, "dev"))
    out_specs = P(None, None, None, None, "dev")
    return jax.shard_map(
        functools.partial(body, devices),
        mesh=mesh,
        in_specs=in_specs,
        out_specs=out_specs,
        check_vma=False,
    )
```

time: 22.3 us -> 21.2 us (0.951)
  Pallas kernels: 21.1 us -> 20 us
    pallas_call x1, Pallas kernels: 21.1 us -> 20 us  [body(): pl.pallas_call(functools.partial(kernel, devices), out_shape=pltpu.VMEM((...]
where the time goes in v3:
time: 21.2 us; the launch traced here: 21.1 us
  Pallas kernels  20 us (94%)
  local copies, waits for them, and re-layouts  1.06 us (5%)
    pallas_call x1, Pallas kernels, body(): pl.pallas_call(functools.partial(kernel, devices), out_shape=pltpu.VMEM((...  20 us
    unnamed x1, local copies, waits for them, and re-layouts  1.06 us

profile of v3, /device:TPU:1, one launch (start us, length us, event | category | flops | bytes accessed | tf_op | source)
XLA Modules:
  0.0 21.1 jit_solution(6770478695709252057)
XLA Ops:
  0.0 20.0 %shard_map.28 = f32[5,8,64,128]{3,2,1,0:T(8,128)S(1)} custom-call(f32[5,8,8,8,128]{4,3,2,1,0:T(8,128)} %state_hbm.1, s32[6,128]{1,0:T(8,128)} %neighbours_hbm.1), custom_call_target="tpu_custom_call" | custom-call | flops 25000000 | bytes 2700000 | tf_op jit(solution)/shard_map/pallas_call | solution.py:388
  20.0 1.1 %copy.4 = f32[5,8,8,8,128]{4,3,2,1,0:T(8,128)} copy(f32[5,8,8,8,128]{4,3,2,1,0:T(8,128)S(1)} %bitcast.1) | data formatting | bytes 2621440

commit v4 on v3

--- a/solution.py
+++ b/solution.py
@@ -48,6 +48,16 @@
 ODD = 0.5 * (MATRIX[:4, :4] - MATRIX[:4, :3:-1])
 
 
+def plane_matrix():
+    identity = np.eye(NODES)
+    two = np.concatenate([np.kron(MATRIX, identity), np.kron(identity, MATRIX)], axis=1)
+    high = two.astype(np.float32).astype(jnp.bfloat16)
+    low = (two - high.astype(np.float64)).astype(np.float32).astype(jnp.bfloat16)
+    upper = np.concatenate([high, high], axis=1)
+    lower = np.concatenate([low, np.zeros_like(low)], axis=1)
+    return np.concatenate([upper, lower], axis=0)
+
+
 def derivative(values, pairs=(0, 1, 2, 3)):
     even = {j: values[j] + values[LAST - j] for j in pairs}
     odd = {j: values[j] - values[LAST - j] for j in pairs}
@@ -100,11 +110,13 @@
     devices,
     state_hbm,
     neighbours_hbm,
+    matrix_hbm,
     out,
     planes,
     r,
     prim,
     ids_ref,
+    matrix,
     index,
     ends,
     recv_z,
@@ -127,10 +139,12 @@
         k: pltpu.make_async_copy(state_hbm.at[:, :, :, k, :], planes.at[:, k], in_sem.at[k])
         for k in ENDS + MIDDLE
     }
-    for load in loads.values():
-        load.start()
+    for k in ENDS:
+        loads[k].start()
     load_ids = pltpu.make_async_copy(neighbours_hbm, ids_ref, in_sem.at[8])
     load_ids.start()
+    load_matrix = pltpu.make_async_copy(matrix_hbm, matrix, in_sem.at[9])
+    load_matrix.start()
 
     barrier = pltpu.get_barrier_semaphore()
     for other in (above, below, partner):
@@ -199,12 +213,33 @@
             yield c, flux
 
     def in_plane(k):
-        for normal, rows in ((0, rows_i), (1, rows_j)):
-            at = lambda n: (k, rows(n))
-            for c, flux in fluxes(normal, at):
-                rate = derivative(flux)
-                for n in range(8):
-                    r[c, *at(n)] = r[c, *at(n)] + rate[n]
+        pairs = ((0, 1), (2, 3), (4,))
+        whole = pl.ds(0, 64)
+        for group in pairs:
+            columns = []
+            for c in group:
+                tall = []
+                for normal in range(2):
+                    if c == 0:
+                        flux = u[1 + normal, k, whole]
+                    elif c == 4:
+                        flux = prim[4, k, whole] * prim[normal, k, whole]
+                    else:
+                        flux = u[c, k, whole] * prim[normal, k, whole]
+                        if c == 1 + normal:
+                            flux = flux + prim[3, k, whole]
+                    tall.append(flux)
+                high = [flux.astype(jnp.bfloat16) for flux in tall]
+                low = [
+                    (flux - h.astype(jnp.float32)).astype(jnp.bfloat16)
+                    for flux, h in zip(tall, high)
+                ]
+                columns.append(jnp.concatenate(high + low, axis=0))
+            right = columns[0] if len(columns) == 1 else jnp.concatenate(columns, axis=1)
+            both = jnp.dot(matrix[...], right, preferred_element_type=jnp.float32)
+            for n, c in enumerate(group):
+                lanes = slice(n * ELEMS, (n + 1) * ELEMS)
+                r[c, k, whole] += both[:64, lanes] + both[64:, lanes]
 
     def surface_x(k):
         left = [u[c, k, rows_i(LAST)] for c in range(5)]
@@ -259,6 +294,8 @@
         send(0, planes.at[:, 0], recv_z.at[0], below),
         send(1, planes.at[:, LAST], recv_z.at[1], above),
     ]
+    for k in MIDDLE:
+        loads[k].start()
     y_copies = [send_y(0, ENDS)]
 
     load_ids.wait()
@@ -284,6 +321,7 @@
                 r[c, *at(n)] = rate[n]
 
     loop(0, 8, along_k_first)
+    load_matrix.wait()
     for k in ENDS:
         in_plane(k)
         surface_x(k)
@@ -294,19 +332,21 @@
         for i in range(8):
             for c in range(5):
                 ends[s, c, i] = u[c, k, rows_i(i)] + STEP * r[c, k, rows_i(i)]
+
+    loop(1, LAST, in_plane, 6)
+    loop(1, LAST, surface_x, 6)
+    y_copies[1].wait_recv()
+    surface_y(0, MIDDLE)
+    for copy in z_copies[:2]:
+        copy.wait_send()
     z_copies += [
         send(2, ends.at[0], recv_z.at[2], below),
         send(3, ends.at[1], recv_z.at[3], above),
     ]
 
-    loop(1, LAST, in_plane)
-    loop(1, LAST, surface_x, 6)
-    y_copies[1].wait_recv()
-    surface_y(0, MIDDLE)
-
     loop(1, LAST, lambda k: primitives(k, True))
     y_copies.append(send_y(1, MIDDLE))
-    loop(1, LAST, in_plane)
+    loop(1, LAST, in_plane, 6)
 
     def along_k_middle(i):
         at = lambda n: (n, rows_i(i))
@@ -321,7 +361,7 @@
     surface_y(1, MIDDLE)
 
     for copy in z_copies[:2]:
-        copy.wait()
+        copy.wait_recv()
 
     def surface_z_first(i):
         rows = rows_i(i)
@@ -388,13 +428,14 @@
     change = pl.pallas_call(
         functools.partial(kernel, devices),
         out_shape=pltpu.VMEM((5, 8, 64, ELEMS), jnp.float32),
-        in_specs=[pl.BlockSpec(memory_space=pltpu.HBM), pl.BlockSpec(memory_space=pltpu.HBM)],
+        in_specs=[pl.BlockSpec(memory_space=pltpu.HBM)] * 3,
         out_specs=pl.BlockSpec(memory_space=pltpu.VMEM),
         scratch_shapes=[
             pltpu.VMEM((5, 8, 8, 8, ELEMS), jnp.float32),
             field,
             field,
             pltpu.VMEM((6, ELEMS), jnp.int32),
+            pltpu.VMEM((128, 256), jnp.bfloat16),
             pltpu.VMEM((8, 8, ELEMS), jnp.int32),
             pltpu.VMEM((2,) + faces, jnp.float32),
             pltpu.VMEM((4,) + faces, jnp.float32),
@@ -403,7 +444,7 @@
             pltpu.VMEM((2, 2, 5, 6, 8, ELEMS), jnp.float32),
             pltpu.VMEM((2, 2, 5, 2, 8, ELEMS), jnp.float32),
             pltpu.VMEM((2, 2, 5, 6, 8, ELEMS), jnp.float32),
-            pltpu.SemaphoreType.DMA((9,)),
+            pltpu.SemaphoreType.DMA((10,)),
             pltpu.SemaphoreType.DMA((8,)),
             pltpu.SemaphoreType.DMA((8,)),
         ],
@@ -416,6 +457,7 @@
     )(
         pltpu.with_memory_space_constraint(state, pltpu.HBM),
         pltpu.with_memory_space_constraint(neighbours, pltpu.HBM),
+        pltpu.with_memory_space_constraint(jnp.asarray(plane_matrix()), pltpu.HBM),
     )
     return change.reshape(state.shape)
 

time: 21.2 us -> 20.8 us (0.981)
  Pallas kernels: 20 us -> 19.7 us
    pallas_call x1, Pallas kernels: 20 us -> 19.7 us  [body(): pl.pallas_call(functools.partial(kernel, devices), out_shape=pltpu.VMEM((...]
where the time goes in v4:
time: 20.8 us; the launch traced here: 20.7 us
  Pallas kernels  19.7 us (95%)
  local copies, waits for them, and re-layouts  1.06 us (5%)
    pallas_call x1, Pallas kernels, body(): pl.pallas_call(functools.partial(kernel, devices), out_shape=pltpu.VMEM((...  19.7 us
    unnamed x1, local copies, waits for them, and re-layouts  1.06 us

profile of v4, /device:TPU:1, one launch (start us, length us, event | category | flops | bytes accessed | tf_op | source)
XLA Modules:
  0.0 20.7 jit_solution(2510554416110786408)
XLA Ops:
  0.0 19.7 %shard_map.37 = f32[5,8,64,128]{3,2,1,0:T(8,128)S(1)} custom-call(f32[5,8,8,8,128]{4,3,2,1,0:T(8,128)} %state_hbm.1, s32[6,128]{1,0:T(8,128)} %neighbours_hbm.1, bf16[128,256]{1,0:T(8,128)(2,1)} %constant.2.clone.matrix_hbm), custom_call_target="tpu_custom_call" | custom-call | flops 25000000 | bytes 2700000 | tf_op jit(solution)/shard_map/pallas_call | solution.py:428
  19.7 1.1 %copy.5 = f32[5,8,8,8,128]{4,3,2,1,0:T(8,128)} copy(f32[5,8,8,8,128]{4,3,2,1,0:T(8,128)S(1)} %bitcast.1) | data formatting | bytes 2621440
